TPU v7x, 128 devices: a whole 4x4x4 slice. The times are simulated.
128 devices in a mesh: dom: 32 (over x, z, core), grp: 4 (over y).
Axes of the slice: x: 4, y: 4, z: 4, core: 2. Of those that a mesh axis runs over, the one named last changes fastest.
Arguments:
- x_current: bfloat16 [524288, 128], P(('dom', 'grp')), may hold values from -6 to 6
- x_cached: bfloat16 [524288, 128], P(('dom', 'grp')), may hold values from -6 to 6
- w_self: bfloat16 [128, 512], replicated, may hold values from -0.5 to 0.5
- w_neigh: bfloat16 [128, 512], replicated, may hold values from -1 to 1
- bias: float32 [512], replicated, may hold values from -3 to 3
- tile_columns: int32 [4096, 40], P(('dom', 'grp')), may hold values from 0 to 255
- tile_count: int32 [4096], P(('dom', 'grp')), may hold values from 1 to 40, as said below
- adjacency: int32 [4096, 40, 2048], P(('dom', 'grp')), may hold values from 0 to 255, as said below
- degree: int32 [524288], P(('dom', 'grp')), may hold values from 1 to 5128, as said below
- boundary_blocks: int32 [128, 1], P(('dom', 'grp')), may hold values from 0 to 31
Outputs:
- hidden: bfloat16 [524288, 512], P(('dom', 'grp'))
Inputs may be any that keep to these rules, and one draw needn't show every extreme that they name: `tile_count`: every device has a row block with all 40 slots live. `adjacency`: 8 entries of a tile row packed into each word, bit b for column 8 c + b. `degree`: at least the number of ones in the row of the live tiles of the node's row block.
All inputs are finite; a program needn't handle non-finite values.
Results may differ from a plain program's by a relative error of at most 0.0025.
Values may be sent and summed in bfloat16 or wider, within the bound.
A program may use at most 192 MiB of HBM per device.

v0:
```python
import math
import jax
import jax.numpy as jnp
from jax import lax
from jax.sharding import PartitionSpec as P


def on_device(
    x_current,
    x_cached,
    w_self,
    w_neigh,
    bias,
    tile_columns,
    tile_count,
    adjacency,
    degree,
    boundary_blocks,
):
    node_rows, width = x_current.shape
    row_blocks, per_tile = tile_columns.shape
    tile_rows = node_rows // row_blocks
    chosen = x_cached.reshape(row_blocks, tile_rows, width)[boundary_blocks[0]]
    received = lax.all_gather(x_current, "grp", axis=0, tiled=True)
    part_blocks = received.reshape(-1, tile_rows, width)
    partial_value = lax.all_gather(chosen[None, None], "grp", axis=1, tiled=True)
    halo_blocks = lax.all_gather(partial_value, "dom", axis=0, tiled=True)
    block_table = jnp.concatenate([part_blocks, halo_blocks.reshape(-1, tile_rows, width)], axis=0)
    group_size = math.gcd(4, row_blocks)
    turns = row_blocks // group_size
    shifts = jnp.arange(8, dtype=jnp.int32)

    def one_group(pieces):
        columns, counts, packed = pieces
        bit_values = (
            packed.reshape(group_size, per_tile, tile_rows, tile_rows // 8, 1) >> shifts & 1
        )
        live_mask = (jnp.arange(per_tile, dtype=jnp.int32)[None, :] < counts[:, None]).astype(
            jnp.int32
        )
        adjacent = (
            bit_values.reshape(group_size, per_tile, tile_rows, tile_rows)
            * live_mask[:, :, None, None]
        ).astype(jnp.bfloat16)
        gathered = block_table[columns]
        return jnp.einsum("stij,stjf->sif", adjacent, gathered, preferred_element_type=jnp.float32)

    totals = lax.map(
        one_group,
        (
            tile_columns.reshape(turns, group_size, per_tile),
            tile_count.reshape(turns, group_size),
            adjacency.reshape(turns, group_size, per_tile, -1),
        ),
    )
    totals = totals.reshape(node_rows, width)
    average = (totals / degree.astype(jnp.float32)[:, None]).astype(jnp.bfloat16)
    summed = (
        jnp.dot(x_current, w_self, preferred_element_type=jnp.float32)
        + jnp.dot(average, w_neigh, preferred_element_type=jnp.float32)
        + bias
    )
    return jnp.maximum(summed, 0.0).astype(jnp.bfloat16)


def solution(mesh):
    in_specs = (
        P(("dom", "grp"), None),
        P(("dom", "grp"), None),
        P(),
        P(),
        P(),
        P(("dom", "grp"), None),
        P(("dom", "grp")),
        P(("dom", "grp"), None, None),
        P(("dom", "grp")),
        P(("dom", "grp"), None),
    )
    out_specs = P(("dom", "grp"), None)
    return jax.shard_map(
        on_device, mesh=mesh, in_specs=in_specs, out_specs=out_specs, check_vma=False
    )
```

profile of v0, /device:TPU:1, one launch (start us, length us, event | category | flops | bytes accessed | tf_op | source)
XLA Modules:
  0.0 343.1 jit_solution(17156375614477139263)
XLA Ops:
  6.5 0.7 all-gather.5.cloned.1.call-update
  8.0 11.2 %all-gather = bf16[4,128,128]{2,1,0:T(8,128)(2,1)} all-gather(bf16[1,128,128]{2,1,0:T(8,128)(2,1)S(1)} %constant_dynamic-slice_fusion.2), channel_id=2, replica_groups=mesh['dom'=32,'grp'=4] {'grp'}, dimensions={0}, use_global_device_ids=true | all-gather | bytes 163840 | tf_op jit(solution)/shard_map/all_gather | solution.py:26
  19.3 20.7 %copy.16 = s32[32,40,2048]{1,2,0:T(8,128)} copy(s32[32,40,2048]{2,1,0:T(8,128)} %param.19) | data formatting | bytes 20971520 | tf_op args[7]
  40.1 4.4 %fusion.21 = f32[4096,512]{1,0:T(8,128)} fusion(bf16[4096,128]{1,0:T(8,128)(2,1)S(1)} %copy-done.2, bf16[128,512]{1,0:T(8,128)(2,1)S(1)} %copy-done.3), kind=kOutput, calls=%fused_computation.26 | convolution fusion | flops 536870912 | bytes 9568256 | tf_op jit(solution)/shard_map/dot_general | solution.py:59
  44.5 16.1 %all-gather.5.cloned.1.call-done = bf16[16384,128]{1,0:T(8,128)(2,1)} async-done(((bf16[4096,128]{1,0:T(8,128)(2,1)}), bf16[16384,128]{1,0:T(8,128)(2,1)}) %all-gather.5.cloned.1.call-update) | async-done | bytes 4194320 | tf_op jit(solution)/shard_map/all_gather | solution.py:24
  60.6 49.4 %all-gather.7.cloned.1.call-done = bf16[128,128,128]{2,1,0:T(8,128)(2,1)} async-done(((bf16[4,128,128]{2,1,0:T(8,128)(2,1)}), bf16[128,128,128]{2,1,0:T(8,128)(2,1)}) %all-gather.7.cloned.1.call-update) | async-done | bytes 4194320 | tf_op jit(solution)/shard_map/all_gather | solution.py:27
  110.0 7.4 %pad_maximum_fusion = bf16[256,128,128]{2,1,0:T(8,128)(2,1)} fusion(bf16[128,128,128]{2,1,0:T(8,128)(2,1)} %all-gather.7.cloned.1.call-done, bf16[128,128,128]{2,1,0:T(8,128)(2,1)} %bitcast.63), kind=kLoop, calls=%fused_computation.21 | loop fusion | flops 4194304 | bytes 16777216 | tf_op jit(solution)/shard_map/concatenate | solution.py:28
  117.4 210.2 %while.12 = (s32[]{:T(128)}, f32[8,4,128,128]{3,2,1,0:T(8,128)}, s32[8,4,40,2048]{2,3,1,0:T(8,128)}, s32[8,4]{1,0:T(8,128)S(1)}, s32[8,4,40]{2,1,0:T(4,128)}, /*index=5*/bf16[256,128,128]{2,1,0:T(8,128)(2,1)}, s32[]{:T(128)}) while((s32[]{:T(128)}, f32[8,4,128,128]{3,2,1,0:T(8,128)}, s32[8,4,40,2048]{2,3,1,0:T(8,128)}, ...), condition=%wide.region_1.2_spmd.clone, body=%wide.region_0.1_spmd.clone.sunk | while | flops 681576256 | bytes 22556296 | solution.py:48
  117.4 0.7 compare_select_fusion.2
  118.2 11.2 %gather_fusion = bf16[160,128,128]{2,1,0:T(8,128)(2,1)} fusion(bf16[256,128,128]{2,1,0:T(8,128)(2,1)} %get-tuple-element.136, s32[1024]{0:T(1024)S(1)} %pad_clamp_fusion.2), kind=kCustom, calls=%fused_computation.clone.clone.1 | custom fusion | bytes 10486400 | tf_op jit(solution)/shard_map/while/body/eval_jaxpr/gather | solution.py:45
  129.3 4.5 %constant_dynamic-slice_fusion.4 = s32[1,4,40,2048]{2,3,1,0:T(8,128)} fusion(s32[8,4,40,2048]{2,3,1,0:T(8,128)} %get-tuple-element.133, s32[]{:T(128)} %get-tuple-element.124), kind=kLoop, calls=%fused_computation.18.clone.1 | loop fusion | bytes 2621444 | tf_op jit(solution)/shard_map/while/body/jit(dynamic_index_in_dim)/dynamic_slice | solution.py:48
  133.8 3.4 copy.20
  137.4 6.3 %fusion.36 = f32[8,4,128,128]{3,2,1,0:T(8,128)} fusion(f32[8,4,128,128]{3,2,1,0:T(8,128)} %get-tuple-element.125, s32[]{:T(128)} %get-tuple-element.124, bf16[4,40,128,128]{3,2,1,0:T(8,128)(2,1)} %bitcast.61, s32[4,40]{1,0:T(4,128)S(1)} %fusion.35, s32[128]{0:T(128)S(1)} %shift_right_arithmetic.64, s32[4,40,128,16]{2,3,1,0:T(8,128)S(1)} %copy.20), kind=kOutput, calls=%fused_computation.12.clone.1 | convolution fusion | flops 681574400 | bytes 6817408 | tf_op jit(solution)/shard_map/while/body/eval_jaxpr/stij,stjf->sif/dot_general | solution.py:46
  143.7 0.7 compare_select_fusion.2
  144.4 11.2 %gather_fusion = bf16[160,128,128]{2,1,0:T(8,128)(2,1)} fusion(bf16[256,128,128]{2,1,0:T(8,128)(2,1)} %get-tuple-element.136, s32[1024]{0:T(1024)S(1)} %pad_clamp_fusion.2), kind=kCustom, calls=%fused_computation.clone.clone.1 | custom fusion | bytes 10486400 | tf_op jit(solution)/shard_map/while/body/eval_jaxpr/gather | solution.py:45
  155.6 4.5 %constant_dynamic-slice_fusion.4 = s32[1,4,40,2048]{2,3,1,0:T(8,128)} fusion(s32[8,4,40,2048]{2,3,1,0:T(8,128)} %get-tuple-element.133, s32[]{:T(128)} %get-tuple-element.124), kind=kLoop, calls=%fused_computation.18.clone.1 | loop fusion | bytes 2621444 | tf_op jit(solution)/shard_map/while/body/jit(dynamic_index_in_dim)/dynamic_slice | solution.py:48
  160.1 3.4 copy.20
  163.7 6.3 %fusion.36 = f32[8,4,128,128]{3,2,1,0:T(8,128)} fusion(f32[8,4,128,128]{3,2,1,0:T(8,128)} %get-tuple-element.125, s32[]{:T(128)} %get-tuple-element.124, bf16[4,40,128,128]{3,2,1,0:T(8,128)(2,1)} %bitcast.61, s32[4,40]{1,0:T(4,128)S(1)} %fusion.35, s32[128]{0:T(128)S(1)} %shift_right_arithmetic.64, s32[4,40,128,16]{2,3,1,0:T(8,128)S(1)} %copy.20), kind=kOutput, calls=%fused_computation.12.clone.1 | convolution fusion | flops 681574400 | bytes 6817408 | tf_op jit(solution)/shard_map/while/body/eval_jaxpr/stij,stjf->sif/dot_general | solution.py:46
  169.9 0.7 compare_select_fusion.2
  170.7 11.2 %gather_fusion = bf16[160,128,128]{2,1,0:T(8,128)(2,1)} fusion(bf16[256,128,128]{2,1,0:T(8,128)(2,1)} %get-tuple-element.136, s32[1024]{0:T(1024)S(1)} %pad_clamp_fusion.2), kind=kCustom, calls=%fused_computation.clone.clone.1 | custom fusion | bytes 10486400 | tf_op jit(solution)/shard_map/while/body/eval_jaxpr/gather | solution.py:45
  181.9 4.5 %constant_dynamic-slice_fusion.4 = s32[1,4,40,2048]{2,3,1,0:T(8,128)} fusion(s32[8,4,40,2048]{2,3,1,0:T(8,128)} %get-tuple-element.133, s32[]{:T(128)} %get-tuple-element.124), kind=kLoop, calls=%fused_computation.18.clone.1 | loop fusion | bytes 2621444 | tf_op jit(solution)/shard_map/while/body/jit(dynamic_index_in_dim)/dynamic_slice | solution.py:48
  186.3 3.4 copy.20
  189.9 6.3 %fusion.36 = f32[8,4,128,128]{3,2,1,0:T(8,128)} fusion(f32[8,4,128,128]{3,2,1,0:T(8,128)} %get-tuple-element.125, s32[]{:T(128)} %get-tuple-element.124, bf16[4,40,128,128]{3,2,1,0:T(8,128)(2,1)} %bitcast.61, s32[4,40]{1,0:T(4,128)S(1)} %fusion.35, s32[128]{0:T(128)S(1)} %shift_right_arithmetic.64, s32[4,40,128,16]{2,3,1,0:T(8,128)S(1)} %copy.20), kind=kOutput, calls=%fused_computation.12.clone.1 | convolution fusion | flops 681574400 | bytes 6817408 | tf_op jit(solution)/shard_map/while/body/eval_jaxpr/stij,stjf->sif/dot_general | solution.py:46
  196.2 0.7 compare_select_fusion.2
  197.0 11.2 %gather_fusion = bf16[160,128,128]{2,1,0:T(8,128)(2,1)} fusion(bf16[256,128,128]{2,1,0:T(8,128)(2,1)} %get-tuple-element.136, s32[1024]{0:T(1024)S(1)} %pad_clamp_fusion.2), kind=kCustom, calls=%fused_computation.clone.clone.1 | custom fusion | bytes 10486400 | tf_op jit(solution)/shard_map/while/body/eval_jaxpr/gather | solution.py:45
  208.1 4.5 %constant_dynamic-slice_fusion.4 = s32[1,4,40,2048]{2,3,1,0:T(8,128)} fusion(s32[8,4,40,2048]{2,3,1,0:T(8,128)} %get-tuple-element.133, s32[]{:T(128)} %get-tuple-element.124), kind=kLoop, calls=%fused_computation.18.clone.1 | loop fusion | bytes 2621444 | tf_op jit(solution)/shard_map/while/body/jit(dynamic_index_in_dim)/dynamic_slice | solution.py:48
  212.6 3.4 copy.20
  216.2 6.3 %fusion.36 = f32[8,4,128,128]{3,2,1,0:T(8,128)} fusion(f32[8,4,128,128]{3,2,1,0:T(8,128)} %get-tuple-element.125, s32[]{:T(128)} %get-tuple-element.124, bf16[4,40,128,128]{3,2,1,0:T(8,128)(2,1)} %bitcast.61, s32[4,40]{1,0:T(4,128)S(1)} %fusion.35, s32[128]{0:T(128)S(1)} %shift_right_arithmetic.64, s32[4,40,128,16]{2,3,1,0:T(8,128)S(1)} %copy.20), kind=kOutput, calls=%fused_computation.12.clone.1 | convolution fusion | flops 681574400 | bytes 6817408 | tf_op jit(solution)/shard_map/while/body/eval_jaxpr/stij,stjf->sif/dot_general | solution.py:46
  222.5 0.7 compare_select_fusion.2
  223.2 11.2 %gather_fusion = bf16[160,128,128]{2,1,0:T(8,128)(2,1)} fusion(bf16[256,128,128]{2,1,0:T(8,128)(2,1)} %get-tuple-element.136, s32[1024]{0:T(1024)S(1)} %pad_clamp_fusion.2), kind=kCustom, calls=%fused_computation.clone.clone.1 | custom fusion | bytes 10486400 | tf_op jit(solution)/shard_map/while/body/eval_jaxpr/gather | solution.py:45
  234.4 4.5 %constant_dynamic-slice_fusion.4 = s32[1,4,40,2048]{2,3,1,0:T(8,128)} fusion(s32[8,4,40,2048]{2,3,1,0:T(8,128)} %get-tuple-element.133, s32[]{:T(128)} %get-tuple-element.124), kind=kLoop, calls=%fused_computation.18.clone.1 | loop fusion | bytes 2621444 | tf_op jit(solution)/shard_map/while/body/jit(dynamic_index_in_dim)/dynamic_slice | solution.py:48
  238.9 3.4 copy.20
  242.4 6.3 %fusion.36 = f32[8,4,128,128]{3,2,1,0:T(8,128)} fusion(f32[8,4,128,128]{3,2,1,0:T(8,128)} %get-tuple-element.125, s32[]{:T(128)} %get-tuple-element.124, bf16[4,40,128,128]{3,2,1,0:T(8,128)(2,1)} %bitcast.61, s32[4,40]{1,0:T(4,128)S(1)} %fusion.35, s32[128]{0:T(128)S(1)} %shift_right_arithmetic.64, s32[4,40,128,16]{2,3,1,0:T(8,128)S(1)} %copy.20), kind=kOutput, calls=%fused_computation.12.clone.1 | convolution fusion | flops 681574400 | bytes 6817408 | tf_op jit(solution)/shard_map/while/body/eval_jaxpr/stij,stjf->sif/dot_general | solution.py:46
  248.7 0.7 compare_select_fusion.2
  249.5 11.2 %gather_fusion = bf16[160,128,128]{2,1,0:T(8,128)(2,1)} fusion(bf16[256,128,128]{2,1,0:T(8,128)(2,1)} %get-tuple-element.136, s32[1024]{0:T(1024)S(1)} %pad_clamp_fusion.2), kind=kCustom, calls=%fused_computation.clone.clone.1 | custom fusion | bytes 10486400 | tf_op jit(solution)/shard_map/while/body/eval_jaxpr/gather | solution.py:45
  260.7 4.5 %constant_dynamic-slice_fusion.4 = s32[1,4,40,2048]{2,3,1,0:T(8,128)} fusion(s32[8,4,40,2048]{2,3,1,0:T(8,128)} %get-tuple-element.133, s32[]{:T(128)} %get-tuple-element.124), kind=kLoop, calls=%fused_computation.18.clone.1 | loop fusion | bytes 2621444 | tf_op jit(solution)/shard_map/while/body/jit(dynamic_index_in_dim)/dynamic_slice | solution.py:48
  265.1 3.4 copy.20
  268.7 6.3 %fusion.36 = f32[8,4,128,128]{3,2,1,0:T(8,128)} fusion(f32[8,4,128,128]{3,2,1,0:T(8,128)} %get-tuple-element.125, s32[]{:T(128)} %get-tuple-element.124, bf16[4,40,128,128]{3,2,1,0:T(8,128)(2,1)} %bitcast.61, s32[4,40]{1,0:T(4,128)S(1)} %fusion.35, s32[128]{0:T(128)S(1)} %shift_right_arithmetic.64, s32[4,40,128,16]{2,3,1,0:T(8,128)S(1)} %copy.20), kind=kOutput, calls=%fused_computation.12.clone.1 | convolution fusion | flops 681574400 | bytes 6817408 | tf_op jit(solution)/shard_map/while/body/eval_jaxpr/stij,stjf->sif/dot_general | solution.py:46
  275.8 11.2 %gather_fusion = bf16[160,128,128]{2,1,0:T(8,128)(2,1)} fusion(bf16[256,128,128]{2,1,0:T(8,128)(2,1)} %get-tuple-element.136, s32[1024]{0:T(1024)S(1)} %pad_clamp_fusion.2), kind=kCustom, calls=%fused_computation.clone.clone.1 | custom fusion | bytes 10486400 | tf_op jit(solution)/shard_map/while/body/eval_jaxpr/gather | solution.py:45
  286.9 4.5 %constant_dynamic-slice_fusion.4 = s32[1,4,40,2048]{2,3,1,0:T(8,128)} fusion(s32[8,4,40,2048]{2,3,1,0:T(8,128)} %get-tuple-element.133, s32[]{:T(128)} %get-tuple-element.124), kind=kLoop, calls=%fused_computation.18.clone.1 | loop fusion | bytes 2621444 | tf_op jit(solution)/shard_map/while/body/jit(dynamic_index_in_dim)/dynamic_slice | solution.py:48
  291.4 3.4 copy.20
  295.0 6.3 %fusion.36 = f32[8,4,128,128]{3,2,1,0:T(8,128)} fusion(f32[8,4,128,128]{3,2,1,0:T(8,128)} %get-tuple-element.125, s32[]{:T(128)} %get-tuple-element.124, bf16[4,40,128,128]{3,2,1,0:T(8,128)(2,1)} %bitcast.61, s32[4,40]{1,0:T(4,128)S(1)} %fusion.35, s32[128]{0:T(128)S(1)} %shift_right_arithmetic.64, s32[4,40,128,16]{2,3,1,0:T(8,128)S(1)} %copy.20), kind=kOutput, calls=%fused_computation.12.clone.1 | convolution fusion | flops 681574400 | bytes 6817408 | tf_op jit(solution)/shard_map/while/body/eval_jaxpr/stij,stjf->sif/dot_general | solution.py:46
  302.1 11.2 %gather_fusion = bf16[160,128,128]{2,1,0:T(8,128)(2,1)} fusion(bf16[256,128,128]{2,1,0:T(8,128)(2,1)} %get-tuple-element.136, s32[1024]{0:T(1024)S(1)} %pad_clamp_fusion.2), kind=kCustom, calls=%fused_computation.clone.clone.1 | custom fusion | bytes 10486400 | tf_op jit(solution)/shard_map/while/body/eval_jaxpr/gather | solution.py:45
  313.2 4.5 %constant_dynamic-slice_fusion.4 = s32[1,4,40,2048]{2,3,1,0:T(8,128)} fusion(s32[8,4,40,2048]{2,3,1,0:T(8,128)} %get-tuple-element.133, s32[]{:T(128)} %get-tuple-element.124), kind=kLoop, calls=%fused_computation.18.clone.1 | loop fusion | bytes 2621444 | tf_op jit(solution)/shard_map/while/body/jit(dynamic_index_in_dim)/dynamic_slice | solution.py:48
  317.7 3.4 copy.20
  321.3 6.3 %fusion.36 = f32[8,4,128,128]{3,2,1,0:T(8,128)} fusion(f32[8,4,128,128]{3,2,1,0:T(8,128)} %get-tuple-element.125, s32[]{:T(128)} %get-tuple-element.124, bf16[4,40,128,128]{3,2,1,0:T(8,128)(2,1)} %bitcast.61, s32[4,40]{1,0:T(4,128)S(1)} %fusion.35, s32[128]{0:T(128)S(1)} %shift_right_arithmetic.64, s32[4,40,128,16]{2,3,1,0:T(8,128)S(1)} %copy.20), kind=kOutput, calls=%fused_computation.12.clone.1 | convolution fusion | flops 681574400 | bytes 6817408 | tf_op jit(solution)/shard_map/while/body/eval_jaxpr/stij,stjf->sif/dot_general | solution.py:46
  327.5 2.0 fusion.20
  329.6 6.6 %maximum_convert_fusion = bf16[4096,512]{1,0:T(8,128)(2,1)} fusion(f32[4096,512]{1,0:T(8,128)} %fusion.21, bf16[4096,128]{1,0:T(8,128)(2,1)S(1)} %fusion.20, bf16[128,512]{1,0:T(8,128)(2,1)S(1)} %copy-done.4, f32[512]{0:T(512)S(1)} %copy-done.6), kind=kOutput, calls=%fused_computation.22 | convolution fusion | flops 545259520 | bytes 13764608 | tf_op jit(solution)/shard_map/dot_general | solution.py:60
  (73 shorter events, 3.7 us)
Async XLA Ops:
  6.5 1.4 copy-start
  6.5 54.0 %all-gather.5.cloned.1.call-start = ((), (), s32[]{:S(2)}) async-start(), calls=%async_computation | async-start | bytes 5242880 | tf_op jit(solution)/shard_map/all_gather | solution.py:24
  7.3 102.7 %all-gather.7.cloned.1.call-start = ((), (), s32[]{:S(2)}) async-start(), calls=%async_computation.1 | async-start | bytes 4325376 | tf_op jit(solution)/shard_map/all_gather | solution.py:27
  19.2 20.7 %copy-start.7 = (s32[32]{0:T(128)S(1)}, s32[32]{0:T(128)}, u32[]{:S(2)}) copy-start(s32[32]{0:T(128)} %param.18) | copy-start | bytes 388
  19.2 20.8 %copy-start.5 = (s32[4096]{0:T(1024)S(1)}, s32[4096]{0:T(1024)}, u32[]{:S(2)}) copy-start(s32[4096]{0:T(1024)} %param.20) | copy-start | bytes 49156
  19.2 20.8 %copy-start.2 = (bf16[4096,128]{1,0:T(8,128)(2,1)S(1)}, bf16[4096,128]{1,0:T(8,128)(2,1)}, u32[]{:S(2)}) copy-start(bf16[4096,128]{1,0:T(8,128)(2,1)} %param.12) | copy-start | bytes 3145732
  19.2 20.8 %copy-start.3 = (bf16[128,512]{1,0:T(8,128)(2,1)S(1)}, bf16[128,512]{1,0:T(8,128)(2,1)}, u32[]{:S(2)}) copy-start(bf16[128,512]{1,0:T(8,128)(2,1)} %param.14) | copy-start | bytes 393220
  117.4 212.2 %copy-start.4 = (bf16[128,512]{1,0:T(8,128)(2,1)S(1)}, bf16[128,512]{1,0:T(8,128)(2,1)}, u32[]{:S(2)}) copy-start(bf16[128,512]{1,0:T(8,128)(2,1)} %param.15) | copy-start | bytes 393220
  117.4 212.2 %copy-start.6 = (f32[512]{0:T(512)S(1)}, f32[512]{0:T(512)}, u32[]{:S(2)}) copy-start(f32[512]{0:T(512)} %param.16) | copy-start | bytes 6148
  327.5 8.7 %copy-start.1 = (bf16[4096,128]{1,0:T(8,128)(2,1)S(1)}, bf16[4096,128]{1,0:T(8,128)(2,1)}, u32[]{:S(2)}) copy-start(bf16[4096,128]{1,0:T(8,128)(2,1)} %param.13) | copy-start | bytes 3145732
Sparse Core Ops, SparseCore 0:
  9.0 51.4 all-gather.4
  62.8 47.1 all-gather.6
where the time goes:
time: 345 us; the launch traced here: 343 us
  local copies, waits for them, and re-layouts  174 us (50%)
  waiting for transfers between devices  66.2 us (19%)
  matrix products  61.2 us (18%)
  other arithmetic  15.6 us (5%)
  between operations  14.2 us (4%)
  blocking collectives  11.2 us (3%)
    gather x8, local copies, waits for them, and re-layouts, one_group(): gathered = block_table[columns]  89.3 us
    dot_general x8, matrix products, one_group(): jnp.einsum('stij,stjf->sif', adjacent, gathered, preferred_element_type=j...  50.2 us
    all_gather x1, waiting for transfers between devices, on_device(): halo_blocks = lax.all_gather(partial_value, 'dom', axis=0, tiled=True)  49.4 us
    dynamic_slice x8, local copies, waits for them, and re-layouts, on_device(): lax.map(one_group, (tile_columns.reshape(turns, group_size, per_tile), ti...  35.8 us
    shift_right_arithmetic x24, local copies, waits for them, and re-layouts, one_group(): packed.reshape(group_size, per_tile, tile_rows, tile_rows // 8, 1) >> shifts  27.9 us
    unnamed x17, local copies, waits for them, and re-layouts  20.7 us
    all_gather x1, waiting for transfers between devices, on_device(): received = lax.all_gather(x_current, 'grp', axis=0, tiled=True)  16.1 us
    all_gather x1, blocking collectives, on_device(): lax.all_gather(chosen[None, None], 'grp', axis=1, tiled=True)  11.2 us
  transfers between devices with their start and end apart: 2, of which 2 were waited for; matrix products, arithmetic and copies ran while one was open for 7% of the time, Pallas kernels for 0%

commit v1 on v0

--- a/solution.py
+++ b/solution.py
@@ -3,6 +3,19 @@
 import jax.numpy as jnp
 from jax import lax
 from jax.sharding import PartitionSpec as P
+
+
+def ring_gather(x, axis, dim):
+    ways = lax.axis_size(axis)
+    up = [(d, (d + 1) % ways) for d in range(ways)]
+    down = [(d, (d - 1) % ways) for d in range(ways)]
+    earlier, later = ([x], [x])
+    for _ in range(ways // 2):
+        earlier.append(lax.ppermute(earlier[-1], axis, up))
+    for _ in range((ways - 1) // 2):
+        later.append(lax.ppermute(later[-1], axis, down))
+    line = jnp.concatenate([*earlier[::-1], *later[1:]], axis=dim)
+    return jnp.roll(line, (lax.axis_index(axis) - ways // 2) * x.shape[dim], axis=dim)
 
 
 def on_device(
@@ -21,7 +34,7 @@
     row_blocks, per_tile = tile_columns.shape
     tile_rows = node_rows // row_blocks
     chosen = x_cached.reshape(row_blocks, tile_rows, width)[boundary_blocks[0]]
-    received = lax.all_gather(x_current, "grp", axis=0, tiled=True)
+    received = ring_gather(x_current, "grp", 0)
     part_blocks = received.reshape(-1, tile_rows, width)
     partial_value = lax.all_gather(chosen[None, None], "grp", axis=1, tiled=True)
     halo_blocks = lax.all_gather(partial_value, "dom", axis=0, tiled=True)

time: 345 us -> 314 us (0.910); the launches traced: 343 us -> 308 us
  waiting for transfers between devices: 66.2 us -> 21.5 us
  local copies, waits for them, and re-layouts: 174 us -> 180 us
  starting transfers between devices: 0.04 us -> 3.75 us
    all_gather x1, waiting for transfers between devices: 49.4 us -> 0.01 us  [on_device(): halo_blocks = lax.all_gather(partial_value, 'dom', axis=0, tiled=True)]
    ppermute x0 -> x3, waiting for transfers between devices: none -> 21.5 us  [the longest x2 21.5 us: ring_gather(): earlier.append(lax.ppermute(earlier[-1], axis, up))]
    all_gather x1 -> x0, waiting for transfers between devices: 16.1 us -> none  [on_device(): received = lax.all_gather(x_current, 'grp', axis=0, tiled=True)]
    ppermute x0 -> x3, starting transfers between devices: none -> 3.75 us  [the longest x1 2.67 us: ring_gather(): later.append(lax.ppermute(later[-1], axis, down))]
    unnamed x17 -> x24, local copies, waits for them, and re-layouts: 20.7 us -> 24.3 us
  transfers between devices with their start and end apart: 2 -> 4, of which waited for: 2 -> 1; matrix products, arithmetic and copies ran while one was open for 7% -> 10% of each run, Pallas kernels for 0% -> 0%
where the time goes in v1:
time: 314 us; the launch traced here: 308 us
  local copies, waits for them, and re-layouts  180 us (57%)
  matrix products  61.1 us (19%)
  waiting for transfers between devices  21.5 us (7%)
  other arithmetic  15.6 us (5%)
  between operations  14.3 us (5%)
  blocking collectives  11.2 us (4%)
  starting transfers between devices  3.75 us (1%)
    gather x8, local copies, waits for them, and re-layouts, one_group(): gathered = block_table[columns]  89.3 us
    dot_general x8, matrix products, one_group(): jnp.einsum('stij,stjf->sif', adjacent, gathered, preferred_element_type=j...  50.1 us
    dynamic_slice x8, local copies, waits for them, and re-layouts, on_device(): lax.map(one_group, (tile_columns.reshape(turns, group_size, per_tile), ti...  35.8 us
    shift_right_arithmetic x24, local copies, waits for them, and re-layouts, one_group(): packed.reshape(group_size, per_tile, tile_rows, tile_rows // 8, 1) >> shifts  27.9 us
    unnamed x24, local copies, waits for them, and re-layouts  24.3 us
    ppermute x2, waiting for transfers between devices, ring_gather(): earlier.append(lax.ppermute(earlier[-1], axis, up))  21.5 us
    all_gather x1, blocking collectives, on_device(): lax.all_gather(chosen[None, None], 'grp', axis=1, tiled=True)  11.2 us
    concatenate x1, other arithmetic, on_device(): jnp.concatenate([part_blocks, halo_blocks.reshape(-1, tile_rows, width)],...  7.4 us
  transfers between devices with their start and end apart: 4, of which 1 were waited for; matrix products, arithmetic and copies ran while one was open for 10% of the time, Pallas kernels for 0%

profile of v1, /device:TPU:1, one launch (start us, length us, event | category | flops | bytes accessed | tf_op | source)
XLA Modules:
  0.0 308.0 jit_solution(682831116496994700)
XLA Ops:
  7.8 11.2 %all-gather = bf16[4,128,128]{2,1,0:T(8,128)(2,1)} all-gather(bf16[1,128,128]{2,1,0:T(8,128)(2,1)S(1)} %constant_dynamic-slice_fusion.2), channel_id=2, replica_groups=mesh['dom'=32,'grp'=4] {'grp'}, dimensions={0}, use_global_device_ids=true | all-gather | bytes 163840 | tf_op jit(solution)/shard_map/all_gather | solution.py:39
  19.0 1.1 collective-permute-start
  20.1 21.5 %collective-permute-done = bf16[4096,128]{1,0:T(8,128)(2,1)S(1)} collective-permute-done((bf16[4096,128]{1,0:T(8,128)(2,1)}, bf16[4096,128]{1,0:T(8,128)(2,1)S(1)}, u32[]{:S(2)}, u32[]{:S(2)}) %collective-permute-start) | collective-permute-done | bytes 1048608 | tf_op jit(solution)/shard_map/ppermute | solution.py:14
  41.6 2.7 collective-permute-start.2
  44.3 20.5 %copy.16 = s32[32,40,2048]{1,2,0:T(8,128)} copy(s32[32,40,2048]{2,1,0:T(8,128)} %param.19) | data formatting | bytes 20971520 | tf_op args[7]
  64.8 4.4 %fusion.21 = f32[4096,512]{1,0:T(8,128)} fusion(bf16[4096,128]{1,0:T(8,128)(2,1)S(1)} %copy-done.2, bf16[128,512]{1,0:T(8,128)(2,1)S(1)} %copy-done.3), kind=kOutput, calls=%fused_computation.35 | convolution fusion | flops 536870912 | bytes 9568256 | tf_op jit(solution)/shard_map/dot_general | solution.py:72
  69.3 1.3 constant_dynamic-update-slice_fusion.7
  71.0 1.4 constant_dynamic-update-slice_fusion.3
  72.8 2.2 constant_dynamic-slice_fusion.3
  75.0 7.4 %pad_maximum_fusion = bf16[256,128,128]{2,1,0:T(8,128)(2,1)} fusion(bf16[128,128,128]{2,1,0:T(8,128)(2,1)} %all-gather.4.cloned.1.call-done, bf16[128,128,128]{2,1,0:T(8,128)(2,1)} %bitcast.63), kind=kLoop, calls=%fused_computation.21 | loop fusion | flops 4194304 | bytes 16777216 | tf_op jit(solution)/shard_map/concatenate | solution.py:41
  82.4 210.1 %while.12 = (s32[]{:T(128)}, f32[8,4,128,128]{3,2,1,0:T(8,128)}, s32[8,4,40,2048]{2,3,1,0:T(8,128)}, s32[8,4]{1,0:T(8,128)S(1)}, s32[8,4,40]{2,1,0:T(4,128)}, /*index=5*/bf16[256,128,128]{2,1,0:T(8,128)(2,1)}, s32[]{:T(128)}) while((s32[]{:T(128)}, f32[8,4,128,128]{3,2,1,0:T(8,128)}, s32[8,4,40,2048]{2,3,1,0:T(8,128)}, ...), condition=%wide.region_1.2_spmd.clone, body=%wide.region_0.1_spmd.clone.sunk | while | flops 681576256 | bytes 22556296 | solution.py:61
  82.4 0.7 compare_select_fusion.2
  83.2 11.2 %gather_fusion = bf16[160,128,128]{2,1,0:T(8,128)(2,1)} fusion(bf16[256,128,128]{2,1,0:T(8,128)(2,1)} %get-tuple-element.136, s32[1024]{0:T(1024)S(1)} %pad_clamp_fusion.2), kind=kCustom, calls=%fused_computation.clone.clone.1 | custom fusion | bytes 10486400 | tf_op jit(solution)/shard_map/while/body/eval_jaxpr/gather | solution.py:58
  94.4 4.5 %constant_dynamic-slice_fusion.5 = s32[1,4,40,2048]{2,3,1,0:T(8,128)} fusion(s32[8,4,40,2048]{2,3,1,0:T(8,128)} %get-tuple-element.133, s32[]{:T(128)} %get-tuple-element.124), kind=kLoop, calls=%fused_computation.18.clone.1 | loop fusion | bytes 2621444 | tf_op jit(solution)/shard_map/while/body/jit(dynamic_index_in_dim)/dynamic_slice | solution.py:61
  98.8 3.4 %copy.20 = s32[4,40,128,16]{2,3,1,0:T(8,128)S(1)} copy(s32[4,40,128,16]{1,3,2,0:T(8,128)} %bitcast.60) | data formatting | bytes 2621440 | tf_op jit(solution)/shard_map/while/body/eval_jaxpr/shift_right_arithmetic | solution.py:49
  102.4 6.3 %fusion.36 = f32[8,4,128,128]{3,2,1,0:T(8,128)} fusion(f32[8,4,128,128]{3,2,1,0:T(8,128)} %get-tuple-element.125, s32[]{:T(128)} %get-tuple-element.124, bf16[4,40,128,128]{3,2,1,0:T(8,128)(2,1)} %bitcast.61, s32[4,40]{1,0:T(4,128)S(1)} %fusion.35, s32[128]{0:T(128)S(1)} %shift_right_arithmetic.64, s32[4,40,128,16]{2,3,1,0:T(8,128)S(1)} %copy.20), kind=kOutput, calls=%fused_computation.12.clone.1 | convolution fusion | flops 681574400 | bytes 6817408 | tf_op jit(solution)/shard_map/while/body/eval_jaxpr/stij,stjf->sif/dot_general | solution.py:59
  108.7 0.7 compare_select_fusion.2
  109.5 11.2 %gather_fusion = bf16[160,128,128]{2,1,0:T(8,128)(2,1)} fusion(bf16[256,128,128]{2,1,0:T(8,128)(2,1)} %get-tuple-element.136, s32[1024]{0:T(1024)S(1)} %pad_clamp_fusion.2), kind=kCustom, calls=%fused_computation.clone.clone.1 | custom fusion | bytes 10486400 | tf_op jit(solution)/shard_map/while/body/eval_jaxpr/gather | solution.py:58
  120.6 4.5 %constant_dynamic-slice_fusion.5 = s32[1,4,40,2048]{2,3,1,0:T(8,128)} fusion(s32[8,4,40,2048]{2,3,1,0:T(8,128)} %get-tuple-element.133, s32[]{:T(128)} %get-tuple-element.124), kind=kLoop, calls=%fused_computation.18.clone.1 | loop fusion | bytes 2621444 | tf_op jit(solution)/shard_map/while/body/jit(dynamic_index_in_dim)/dynamic_slice | solution.py:61
  125.1 3.4 %copy.20 = s32[4,40,128,16]{2,3,1,0:T(8,128)S(1)} copy(s32[4,40,128,16]{1,3,2,0:T(8,128)} %bitcast.60) | data formatting | bytes 2621440 | tf_op jit(solution)/shard_map/while/body/eval_jaxpr/shift_right_arithmetic | solution.py:49
  128.7 6.2 %fusion.36 = f32[8,4,128,128]{3,2,1,0:T(8,128)} fusion(f32[8,4,128,128]{3,2,1,0:T(8,128)} %get-tuple-element.125, s32[]{:T(128)} %get-tuple-element.124, bf16[4,40,128,128]{3,2,1,0:T(8,128)(2,1)} %bitcast.61, s32[4,40]{1,0:T(4,128)S(1)} %fusion.35, s32[128]{0:T(128)S(1)} %shift_right_arithmetic.64, s32[4,40,128,16]{2,3,1,0:T(8,128)S(1)} %copy.20), kind=kOutput, calls=%fused_computation.12.clone.1 | convolution fusion | flops 681574400 | bytes 6817408 | tf_op jit(solution)/shard_map/while/body/eval_jaxpr/stij,stjf->sif/dot_general | solution.py:59
  135.7 11.2 %gather_fusion = bf16[160,128,128]{2,1,0:T(8,128)(2,1)} fusion(bf16[256,128,128]{2,1,0:T(8,128)(2,1)} %get-tuple-element.136, s32[1024]{0:T(1024)S(1)} %pad_clamp_fusion.2), kind=kCustom, calls=%fused_computation.clone.clone.1 | custom fusion | bytes 10486400 | tf_op jit(solution)/shard_map/while/body/eval_jaxpr/gather | solution.py:58
  146.9 4.5 %constant_dynamic-slice_fusion.5 = s32[1,4,40,2048]{2,3,1,0:T(8,128)} fusion(s32[8,4,40,2048]{2,3,1,0:T(8,128)} %get-tuple-element.133, s32[]{:T(128)} %get-tuple-element.124), kind=kLoop, calls=%fused_computation.18.clone.1 | loop fusion | bytes 2621444 | tf_op jit(solution)/shard_map/while/body/jit(dynamic_index_in_dim)/dynamic_slice | solution.py:61
  151.3 3.4 %copy.20 = s32[4,40,128,16]{2,3,1,0:T(8,128)S(1)} copy(s32[4,40,128,16]{1,3,2,0:T(8,128)} %bitcast.60) | data formatting | bytes 2621440 | tf_op jit(solution)/shard_map/while/body/eval_jaxpr/shift_right_arithmetic | solution.py:49
  154.9 6.2 %fusion.36 = f32[8,4,128,128]{3,2,1,0:T(8,128)} fusion(f32[8,4,128,128]{3,2,1,0:T(8,128)} %get-tuple-element.125, s32[]{:T(128)} %get-tuple-element.124, bf16[4,40,128,128]{3,2,1,0:T(8,128)(2,1)} %bitcast.61, s32[4,40]{1,0:T(4,128)S(1)} %fusion.35, s32[128]{0:T(128)S(1)} %shift_right_arithmetic.64, s32[4,40,128,16]{2,3,1,0:T(8,128)S(1)} %copy.20), kind=kOutput, calls=%fused_computation.12.clone.1 | convolution fusion | flops 681574400 | bytes 6817408 | tf_op jit(solution)/shard_map/while/body/eval_jaxpr/stij,stjf->sif/dot_general | solution.py:59
  162.0 11.2 %gather_fusion = bf16[160,128,128]{2,1,0:T(8,128)(2,1)} fusion(bf16[256,128,128]{2,1,0:T(8,128)(2,1)} %get-tuple-element.136, s32[1024]{0:T(1024)S(1)} %pad_clamp_fusion.2), kind=kCustom, calls=%fused_computation.clone.clone.1 | custom fusion | bytes 10486400 | tf_op jit(solution)/shard_map/while/body/eval_jaxpr/gather | solution.py:58
  173.1 4.5 %constant_dynamic-slice_fusion.5 = s32[1,4,40,2048]{2,3,1,0:T(8,128)} fusion(s32[8,4,40,2048]{2,3,1,0:T(8,128)} %get-tuple-element.133, s32[]{:T(128)} %get-tuple-element.124), kind=kLoop, calls=%fused_computation.18.clone.1 | loop fusion | bytes 2621444 | tf_op jit(solution)/shard_map/while/body/jit(dynamic_index_in_dim)/dynamic_slice | solution.py:61
  177.6 3.4 %copy.20 = s32[4,40,128,16]{2,3,1,0:T(8,128)S(1)} copy(s32[4,40,128,16]{1,3,2,0:T(8,128)} %bitcast.60) | data formatting | bytes 2621440 | tf_op jit(solution)/shard_map/while/body/eval_jaxpr/shift_right_arithmetic | solution.py:49
  181.2 6.3 %fusion.36 = f32[8,4,128,128]{3,2,1,0:T(8,128)} fusion(f32[8,4,128,128]{3,2,1,0:T(8,128)} %get-tuple-element.125, s32[]{:T(128)} %get-tuple-element.124, bf16[4,40,128,128]{3,2,1,0:T(8,128)(2,1)} %bitcast.61, s32[4,40]{1,0:T(4,128)S(1)} %fusion.35, s32[128]{0:T(128)S(1)} %shift_right_arithmetic.64, s32[4,40,128,16]{2,3,1,0:T(8,128)S(1)} %copy.20), kind=kOutput, calls=%fused_computation.12.clone.1 | convolution fusion | flops 681574400 | bytes 6817408 | tf_op jit(solution)/shard_map/while/body/eval_jaxpr/stij,stjf->sif/dot_general | solution.py:59
  187.4 0.7 compare_select_fusion.2
  188.2 11.2 %gather_fusion = bf16[160,128,128]{2,1,0:T(8,128)(2,1)} fusion(bf16[256,128,128]{2,1,0:T(8,128)(2,1)} %get-tuple-element.136, s32[1024]{0:T(1024)S(1)} %pad_clamp_fusion.2), kind=kCustom, calls=%fused_computation.clone.clone.1 | custom fusion | bytes 10486400 | tf_op jit(solution)/shard_map/while/body/eval_jaxpr/gather | solution.py:58
  199.4 4.5 %constant_dynamic-slice_fusion.5 = s32[1,4,40,2048]{2,3,1,0:T(8,128)} fusion(s32[8,4,40,2048]{2,3,1,0:T(8,128)} %get-tuple-element.133, s32[]{:T(128)} %get-tuple-element.124), kind=kLoop, calls=%fused_computation.18.clone.1 | loop fusion | bytes 2621444 | tf_op jit(solution)/shard_map/while/body/jit(dynamic_index_in_dim)/dynamic_slice | solution.py:61
  203.8 3.4 %copy.20 = s32[4,40,128,16]{2,3,1,0:T(8,128)S(1)} copy(s32[4,40,128,16]{1,3,2,0:T(8,128)} %bitcast.60) | data formatting | bytes 2621440 | tf_op jit(solution)/shard_map/while/body/eval_jaxpr/shift_right_arithmetic | solution.py:49
  207.4 6.3 %fusion.36 = f32[8,4,128,128]{3,2,1,0:T(8,128)} fusion(f32[8,4,128,128]{3,2,1,0:T(8,128)} %get-tuple-element.125, s32[]{:T(128)} %get-tuple-element.124, bf16[4,40,128,128]{3,2,1,0:T(8,128)(2,1)} %bitcast.61, s32[4,40]{1,0:T(4,128)S(1)} %fusion.35, s32[128]{0:T(128)S(1)} %shift_right_arithmetic.64, s32[4,40,128,16]{2,3,1,0:T(8,128)S(1)} %copy.20), kind=kOutput, calls=%fused_computation.12.clone.1 | convolution fusion | flops 681574400 | bytes 6817408 | tf_op jit(solution)/shard_map/while/body/eval_jaxpr/stij,stjf->sif/dot_general | solution.py:59
  214.5 11.2 %gather_fusion = bf16[160,128,128]{2,1,0:T(8,128)(2,1)} fusion(bf16[256,128,128]{2,1,0:T(8,128)(2,1)} %get-tuple-element.136, s32[1024]{0:T(1024)S(1)} %pad_clamp_fusion.2), kind=kCustom, calls=%fused_computation.clone.clone.1 | custom fusion | bytes 10486400 | tf_op jit(solution)/shard_map/while/body/eval_jaxpr/gather | solution.py:58
  225.6 4.5 %constant_dynamic-slice_fusion.5 = s32[1,4,40,2048]{2,3,1,0:T(8,128)} fusion(s32[8,4,40,2048]{2,3,1,0:T(8,128)} %get-tuple-element.133, s32[]{:T(128)} %get-tuple-element.124), kind=kLoop, calls=%fused_computation.18.clone.1 | loop fusion | bytes 2621444 | tf_op jit(solution)/shard_map/while/body/jit(dynamic_index_in_dim)/dynamic_slice | solution.py:61
  230.1 3.4 %copy.20 = s32[4,40,128,16]{2,3,1,0:T(8,128)S(1)} copy(s32[4,40,128,16]{1,3,2,0:T(8,128)} %bitcast.60) | data formatting | bytes 2621440 | tf_op jit(solution)/shard_map/while/body/eval_jaxpr/shift_right_arithmetic | solution.py:49
  233.7 6.3 %fusion.36 = f32[8,4,128,128]{3,2,1,0:T(8,128)} fusion(f32[8,4,128,128]{3,2,1,0:T(8,128)} %get-tuple-element.125, s32[]{:T(128)} %get-tuple-element.124, bf16[4,40,128,128]{3,2,1,0:T(8,128)(2,1)} %bitcast.61, s32[4,40]{1,0:T(4,128)S(1)} %fusion.35, s32[128]{0:T(128)S(1)} %shift_right_arithmetic.64, s32[4,40,128,16]{2,3,1,0:T(8,128)S(1)} %copy.20), kind=kOutput, calls=%fused_computation.12.clone.1 | convolution fusion | flops 681574400 | bytes 6817408 | tf_op jit(solution)/shard_map/while/body/eval_jaxpr/stij,stjf->sif/dot_general | solution.py:59
  240.7 11.2 %gather_fusion = bf16[160,128,128]{2,1,0:T(8,128)(2,1)} fusion(bf16[256,128,128]{2,1,0:T(8,128)(2,1)} %get-tuple-element.136, s32[1024]{0:T(1024)S(1)} %pad_clamp_fusion.2), kind=kCustom, calls=%fused_computation.clone.clone.1 | custom fusion | bytes 10486400 | tf_op jit(solution)/shard_map/while/body/eval_jaxpr/gather | solution.py:58
  251.9 4.5 %constant_dynamic-slice_fusion.5 = s32[1,4,40,2048]{2,3,1,0:T(8,128)} fusion(s32[8,4,40,2048]{2,3,1,0:T(8,128)} %get-tuple-element.133, s32[]{:T(128)} %get-tuple-element.124), kind=kLoop, calls=%fused_computation.18.clone.1 | loop fusion | bytes 2621444 | tf_op jit(solution)/shard_map/while/body/jit(dynamic_index_in_dim)/dynamic_slice | solution.py:61
  256.4 3.4 %copy.20 = s32[4,40,128,16]{2,3,1,0:T(8,128)S(1)} copy(s32[4,40,128,16]{1,3,2,0:T(8,128)} %bitcast.60) | data formatting | bytes 2621440 | tf_op jit(solution)/shard_map/while/body/eval_jaxpr/shift_right_arithmetic | solution.py:49
  260.0 6.3 %fusion.36 = f32[8,4,128,128]{3,2,1,0:T(8,128)} fusion(f32[8,4,128,128]{3,2,1,0:T(8,128)} %get-tuple-element.125, s32[]{:T(128)} %get-tuple-element.124, bf16[4,40,128,128]{3,2,1,0:T(8,128)(2,1)} %bitcast.61, s32[4,40]{1,0:T(4,128)S(1)} %fusion.35, s32[128]{0:T(128)S(1)} %shift_right_arithmetic.64, s32[4,40,128,16]{2,3,1,0:T(8,128)S(1)} %copy.20), kind=kOutput, calls=%fused_computation.12.clone.1 | convolution fusion | flops 681574400 | bytes 6817408 | tf_op jit(solution)/shard_map/while/body/eval_jaxpr/stij,stjf->sif/dot_general | solution.py:59
  267.0 11.2 %gather_fusion = bf16[160,128,128]{2,1,0:T(8,128)(2,1)} fusion(bf16[256,128,128]{2,1,0:T(8,128)(2,1)} %get-tuple-element.136, s32[1024]{0:T(1024)S(1)} %pad_clamp_fusion.2), kind=kCustom, calls=%fused_computation.clone.clone.1 | custom fusion | bytes 10486400 | tf_op jit(solution)/shard_map/while/body/eval_jaxpr/gather | solution.py:58
  278.2 4.5 %constant_dynamic-slice_fusion.5 = s32[1,4,40,2048]{2,3,1,0:T(8,128)} fusion(s32[8,4,40,2048]{2,3,1,0:T(8,128)} %get-tuple-element.133, s32[]{:T(128)} %get-tuple-element.124), kind=kLoop, calls=%fused_computation.18.clone.1 | loop fusion | bytes 2621444 | tf_op jit(solution)/shard_map/while/body/jit(dynamic_index_in_dim)/dynamic_slice | solution.py:61
  282.6 3.4 %copy.20 = s32[4,40,128,16]{2,3,1,0:T(8,128)S(1)} copy(s32[4,40,128,16]{1,3,2,0:T(8,128)} %bitcast.60) | data formatting | bytes 2621440 | tf_op jit(solution)/shard_map/while/body/eval_jaxpr/shift_right_arithmetic | solution.py:49
  286.2 6.3 %fusion.36 = f32[8,4,128,128]{3,2,1,0:T(8,128)} fusion(f32[8,4,128,128]{3,2,1,0:T(8,128)} %get-tuple-element.125, s32[]{:T(128)} %get-tuple-element.124, bf16[4,40,128,128]{3,2,1,0:T(8,128)(2,1)} %bitcast.61, s32[4,40]{1,0:T(4,128)S(1)} %fusion.35, s32[128]{0:T(128)S(1)} %shift_right_arithmetic.64, s32[4,40,128,16]{2,3,1,0:T(8,128)S(1)} %copy.20), kind=kOutput, calls=%fused_computation.12.clone.1 | convolution fusion | flops 681574400 | bytes 6817408 | tf_op jit(solution)/shard_map/while/body/eval_jaxpr/stij,stjf->sif/dot_general | solution.py:59
  292.5 2.0 fusion.20
  294.5 6.6 %maximum_convert_fusion = bf16[4096,512]{1,0:T(8,128)(2,1)} fusion(f32[4096,512]{1,0:T(8,128)} %fusion.21, bf16[4096,128]{1,0:T(8,128)(2,1)S(1)} %fusion.20, bf16[128,512]{1,0:T(8,128)(2,1)S(1)} %copy-done.4, f32[512]{0:T(512)S(1)} %copy-done.6), kind=kOutput, calls=%fused_computation.22 | convolution fusion | flops 545259520 | bytes 13764608 | tf_op jit(solution)/shard_map/dot_general | solution.py:73
  (85 shorter events, 7.0 us)
Async XLA Ops:
  6.5 1.2 copy-start
  6.5 68.5 %all-gather.4.cloned.1.call-start = ((), (), s32[]{:S(2)}) async-start(), calls=%async_computation | async-start | bytes 4325376 | tf_op jit(solution)/shard_map/all_gather | solution.py:40
  19.0 22.6 %collective-permute-start = (bf16[4096,128]{1,0:T(8,128)(2,1)}, bf16[4096,128]{1,0:T(8,128)(2,1)S(1)}, u32[]{:S(2)}, u32[]{:S(2)}) collective-permute-start(bf16[4096,128]{1,0:T(8,128)(2,1)} %param.12), channel_id=1, source_target_pairs={{0,1},{1,2},{2,3},{3,0},{4,5},{5,6},{6,7},{7,4},{8,9},{9,10},{10,1... | collective-permute-start | bytes 3145736 | tf_op jit(solution)/shard_map/ppermute | solution.py:14
  41.6 27.7 %collective-permute-start.1 = (bf16[4096,128]{1,0:T(8,128)(2,1)S(1)}, bf16[4096,128]{1,0:T(8,128)(2,1)}, u32[]{:S(2)}, u32[]{:S(2)}) collective-permute-start(bf16[4096,128]{1,0:T(8,128)(2,1)S(1)} %collective-permute-done), channel_id=1, source_target_pairs={{0,1},{1,2},{2,3},{3,0},{4,5},{5,6},{6,7},{7,4},{8,9},{9,10},{10,1... | collective-permute-start | bytes 3145736 | tf_op jit(solution)/shard_map/ppermute | solution.py:14
  41.6 29.3 %collective-permute-start.2 = (bf16[4096,128]{1,0:T(8,128)(2,1)}, bf16[4096,128]{1,0:T(8,128)(2,1)S(1)}, u32[]{:S(2)}, u32[]{:S(2)}) collective-permute-start(bf16[4096,128]{1,0:T(8,128)(2,1)} %param.12), channel_id=1, source_target_pairs={{0,3},{1,0},{2,1},{3,2},{4,7},{5,4},{6,5},{7,6},{8,11},{9,8},{10,9... | collective-permute-start | bytes 3145736 | tf_op jit(solution)/shard_map/ppermute | solution.py:16
  44.2 20.5 %copy-start.7 = (s32[32]{0:T(128)S(1)}, s32[32]{0:T(128)}, u32[]{:S(2)}) copy-start(s32[32]{0:T(128)} %param.18) | copy-start | bytes 388
  44.2 20.6 %copy-start.5 = (s32[4096]{0:T(1024)S(1)}, s32[4096]{0:T(1024)}, u32[]{:S(2)}) copy-start(s32[4096]{0:T(1024)} %param.20) | copy-start | bytes 49156
  44.2 20.6 %copy-start.2 = (bf16[4096,128]{1,0:T(8,128)(2,1)S(1)}, bf16[4096,128]{1,0:T(8,128)(2,1)}, u32[]{:S(2)}) copy-start(bf16[4096,128]{1,0:T(8,128)(2,1)} %param.12) | copy-start | bytes 3145732
  44.2 20.6 %copy-start.3 = (bf16[128,512]{1,0:T(8,128)(2,1)S(1)}, bf16[128,512]{1,0:T(8,128)(2,1)}, u32[]{:S(2)}) copy-start(bf16[128,512]{1,0:T(8,128)(2,1)} %param.14) | copy-start | bytes 393220
  82.4 212.1 %copy-start.4 = (bf16[128,512]{1,0:T(8,128)(2,1)S(1)}, bf16[128,512]{1,0:T(8,128)(2,1)}, u32[]{:S(2)}) copy-start(bf16[128,512]{1,0:T(8,128)(2,1)} %param.15) | copy-start | bytes 393220
  82.4 212.1 %copy-start.6 = (f32[512]{0:T(512)S(1)}, f32[512]{0:T(512)}, u32[]{:S(2)}) copy-start(f32[512]{0:T(512)} %param.16) | copy-start | bytes 6148
  292.5 8.7 %copy-start.1 = (bf16[4096,128]{1,0:T(8,128)(2,1)S(1)}, bf16[4096,128]{1,0:T(8,128)(2,1)}, u32[]{:S(2)}) copy-start(bf16[4096,128]{1,0:T(8,128)(2,1)} %param.13) | copy-start | bytes 3145732
Sparse Core Ops, SparseCore 0:
  19.1 51.3 all-gather.3
